TPU v7x, 256 devices: a whole 4x4x8 slice. The times are simulated.
256 devices in a mesh: row: 8 (over y_lo, x), col: 32 (over z, y_hi, core).
Axes of the slice: x: 4, y: 4 (y_hi: 2, y_lo: 2; y = y_hi * 2 + y_lo), z: 8, core: 2. Of those that a mesh axis runs over, the one named last changes fastest.
Arguments:
- left_features: bfloat16 [32, 2048, 320], P('row', 'col'), may hold values from -6 to 6
- right_features: bfloat16 [32, 2048, 320], P('row', 'col'), may hold values from -6 to 6
- conv_weight: bfloat16 [3, 3, 3, 40, 32], replicated, may hold values from -0.1875 to 0.1875
- cotangent: bfloat16 [24, 32, 2048, 32], P(None, 'row', 'col'), may hold values from -6 to 6
Outputs:
- cost_output: bfloat16 [24, 32, 2048, 32], P(None, 'row', 'col')
- weight_grad: float32 [3, 3, 3, 40, 32], replicated
- left_grad: bfloat16 [32, 2048, 320], P('row', 'col')
- right_grad: bfloat16 [32, 2048, 320], P('row', 'col')
All inputs are finite; a program needn't handle non-finite values.
Results may differ from a plain program's by a relative error of at most 0.0049.
Values may be sent and summed in bfloat16 or wider, within the bound.
A program may use at most 128 MiB of HBM per device.

v0:
```python
import math
import jax
import jax.numpy as jnp
from jax import lax
from jax.sharding import PartitionSpec as P

DISP = 24
STEP = 4
DIMS = ("NDHWC", "DHWIO", "NDHWC")
KERNEL_DIMS = ("CDHWN", "IDHWO", "NDHWC")


def shifted_2(block, axis, distance):
    devices = range(lax.axis_size(axis))
    route = [(i - distance, i) for i in devices if i - distance in devices]
    return lax.ppermute(block, axis, route)


def with_halo(cells, sides, width):
    for axis, dim in sides:
        count = lax.axis_size(axis)
        ends = count - 1
        head = lax.slice_in_dim(cells, 0, width, axis=dim)
        tail = lax.slice_in_dim(cells, cells.shape[dim] - width, cells.shape[dim], axis=dim)
        cells = jnp.concatenate(
            [
                lax.ppermute(tail, axis, [(i, (i + 1) % count) for i in range(ends)]),
                cells,
                lax.ppermute(head, axis, [((i + 1) % count, i) for i in range(ends)]),
            ],
            axis=dim,
        )
    return cells


def conv_valid(padded_input, kernel):
    return lax.conv_general_dilated(
        padded_input[None],
        kernel,
        (1, 1, 1),
        ((1, 1), (0, 0), (0, 0)),
        dimension_numbers=DIMS,
        preferred_element_type=jnp.float32,
    )[0]


def on_device(left_features, right_features, conv_weight, cotangent):
    tile_rows, tile_cols, channels = left_features.shape
    groups = conv_weight.shape[3]
    group_size = channels // groups
    reach_cols = STEP * (DISP - 1)
    hop_count = -(-reach_cols // tile_cols)
    band_base = hop_count * tile_cols
    band_width = band_base + tile_cols
    pieces = [right_features]
    carried = right_features
    for hop_index in range(hop_count):
        carried = shifted_2(carried, "col", 1)
        pieces.insert(0, carried)
    right_band = jnp.concatenate(pieces, axis=1)
    group_table = (
        jnp.arange(channels)[:, None] // group_size == jnp.arange(groups)[None, :]
    ).astype(jnp.float32)
    left_float = left_features.astype(jnp.float32)
    planes = []
    for disp_index in range(DISP):
        band_start = band_base - STEP * disp_index
        shifted = right_band[:, band_start : band_start + tile_cols].astype(jnp.float32)
        planes.append(
            jnp.einsum(
                "hwc,cg->hwg", left_float * shifted, group_table, precision=lax.Precision.HIGHEST
            )
        )
    volume = (jnp.stack(planes) / group_size).astype(jnp.bfloat16)
    padded_volume = with_halo(volume, (("row", 1), ("col", 2)), 1)
    output = conv_valid(padded_volume, conv_weight).astype(jnp.bfloat16)
    padded_cotangent = with_halo(cotangent, (("row", 1), ("col", 2)), 1)
    flipped = jnp.transpose(conv_weight[::-1, ::-1, ::-1], (0, 1, 2, 4, 3))
    grad_volume = conv_valid(padded_cotangent, flipped).astype(jnp.bfloat16)
    full_pad = jnp.pad(padded_volume, ((1, 1), (0, 0), (0, 0), (0, 0)))
    kernel_raw = lax.conv_general_dilated(
        full_pad[None],
        cotangent[None],
        (1, 1, 1),
        ((0, 0), (0, 0), (0, 0)),
        dimension_numbers=KERNEL_DIMS,
        preferred_element_type=jnp.float32,
    )
    local_grad = jnp.transpose(kernel_raw, (1, 2, 3, 0, 4))
    total_cells = DISP * tile_rows * lax.axis_size("row") * tile_cols * lax.axis_size("col")
    weight_grad = lax.psum(local_grad, ("row", "col")) / math.sqrt(total_cells)
    left_accum = jnp.zeros((tile_rows, tile_cols, channels), jnp.float32)
    grad_band = jnp.zeros((tile_rows, band_width, channels), jnp.float32)
    for disp_index in range(DISP):
        band_start = band_base - STEP * disp_index
        shifted = right_band[:, band_start : band_start + tile_cols].astype(jnp.float32)
        spread = jnp.einsum(
            "hwg,cg->hwc",
            grad_volume[disp_index].astype(jnp.float32),
            group_table,
            precision=lax.Precision.HIGHEST,
        )
        left_accum = left_accum + spread * shifted
        contrib = spread * left_float
        grad_band = grad_band + jnp.pad(
            contrib, ((0, 0), (band_start, band_width - band_start - tile_cols), (0, 0))
        )

    def band_piece(hop_index):
        return grad_band[
            :, band_base - hop_index * tile_cols : band_base - (hop_index - 1) * tile_cols
        ]

    right_accum = band_piece(hop_count)
    for hop_index in range(hop_count - 1, -1, -1):
        right_accum = shifted_2(right_accum, "col", -1) + band_piece(hop_index)
    left_grad = (left_accum / group_size).astype(jnp.bfloat16)
    right_grad = (right_accum / group_size).astype(jnp.bfloat16)
    return (output, weight_grad, left_grad, right_grad)


def solution(mesh):
    in_specs = (P("row", "col", None), P("row", "col", None), P(), P(None, "row", "col", None))
    out_specs = (P(None, "row", "col", None), P(), P("row", "col", None), P("row", "col", None))
    return jax.shard_map(
        on_device, mesh=mesh, in_specs=in_specs, out_specs=out_specs, check_vma=False
    )
```

profile of v0, /device:TPU:1, one launch (start us, length us, event | category | flops | bytes accessed | tf_op | source)
XLA Modules:
  0.0 492.1 jit_solution(12546032081893617520)
XLA Ops:
  7.2 2.0 copy.212
  9.3 4.1 collective-permute-start.6
  14.7 5.7 %collective-permute-start = (bf16[4,64,320]{2,1,0:T(8,128)(2,1)S(1)}, bf16[4,64,320]{2,1,0:T(8,128)(2,1)}, u32[]{:S(2)}, u32[]{:S(2)}) collective-permute-start(bf16[4,64,320]{2,1,0:T(8,128)(2,1)S(1)} %copy-done.27), channel_id=1, source_target_pairs={{0,1},{1,2},{2,3},{3,4},{4,5},{5,6},{6,7},{7,8},{8,9},{9,10},{10,1... | collective-permute-start | bytes 491528 | tf_op jit(solution)/shard_map/ppermute | solution.py:16
  21.2 3.8 collective-permute-done.7
  25.8 6.6 %collective-permute-start.8 = (bf16[24,6,1,32]{3,0,2,1:T(8,128)(2,1)S(1)}, bf16[24,6,1,32]{3,0,2,1:T(8,128)(2,1)S(1)}, u32[]{:S(2)}, u32[]{:S(2)}) collective-permute-start(bf16[24,6,1,32]{3,0,2,1:T(8,128)(2,1)S(1)} %get-tuple-element.20), channel_id=1, source_target_pairs={{0,1},{1,2},{2,3},{3,4},{4,5},{5,6},{6,7},{7,8},{8,9},{9,10},{10,1... | collective-permute-start | bytes 27656 | tf_op jit(solution)/shard_map/ppermute | solution.py:27
  32.3 1.9 collective-permute-start.9
  35.4 5.1 %copy.211 = bf16[1,24,4,64,32]{4,0,3,2,1:T(2,128)(2,1)} copy(bf16[1,24,4,64,32]{3,4,2,1,0:T(8,128)(2,1)S(1)} %bitcast.279) | data formatting | bytes 786432 | tf_op jit(solution)/shard_map/broadcast_in_dim | solution.py:83
  40.5 2.5 maximum_bitcast_fusion
  44.3 5.4 %select_convert_fusion = bf16[24,4,8,9,40]{4,2,3,1,0:T(8,128)(2,1)S(1)} fusion(pred[8,9]{0,1:T(8,128)(4,1)S(1)} %copy-done.29, bf16[3,3,3,40,32]{3,4,2,1,0:T(8,128)(2,1)S(1)} %copy-done, bf16[24,6,1,7,2,32]{5,3,4,1,0,2:T(8,128)(2,1)S(1)} %slice.377, bf16[24,6,1,8,9,32]{5,3,4,1,0,2:T(8,128)(2,1)S(1)} %copy.216), kind=kOutput, calls=%fused_computation.52 | convolution fusion | flops 467472384 | bytes 1414728 | tf_op jit(solution)/shard_map/conv_general_dilated | solution.py:37
  99.1 6.1 %convert_multiply_fusion.23 = (f32[4,64,320]{2,1,0:T(8,128)}, f32[4,64,320]{2,1,0:T(8,128)}, f32[4,64,320]{2,1,0:T(8,128)}, f32[4,64,320]{2,1,0:T(8,128)}, f32[4...) fusion(bf16[4,64,320]{2,1,0:T(8,128)(2,1)S(1)} %copy-done.1, ...), kind=kOutput, calls=%fused_computation.27 | convolution fusion | flops 8122880 | bytes 11982080 | tf_op jit(solution)/shard_map/hwg,cg->hwc/dot_general | solution.py:97
  105.5 5.7 %collective-permute-start.1 = (bf16[4,64,320]{2,1,0:T(8,128)(2,1)}, bf16[4,64,320]{2,1,0:T(8,128)(2,1)S(1)}, u32[]{:S(2)}, u32[]{:S(2)}) collective-permute-start(bf16[4,64,320]{2,1,0:T(8,128)(2,1)} %collective-permute-done), channel_id=1, source_target_pairs={{0,1},{1,2},{2,3},{3,4},{4,5},{5,6},{6,7},{7,8},{8,9},{9,10},{10,1... | collective-permute-start | bytes 491528 | tf_op jit(solution)/shard_map/ppermute | solution.py:16
  111.4 2.3 collective-permute-done.1
  127.9 3.4 collective-permute-start.2
  132.8 3.0 multiply_convert_fusion.1
  138.6 1.8 fusion.250
  140.4 2.3 copy.202
  142.7 7.6 %collective-permute-start.4 = (bf16[24,6,1,40]{3,0,2,1:T(8,128)(2,1)S(1)}, bf16[24,6,1,40]{3,0,2,1:T(8,128)(2,1)S(1)}, u32[]{:S(2)}, u32[]{:S(2)}) collective-permute-start(bf16[24,6,1,40]{3,0,2,1:T(8,128)(2,1)S(1)} %copy.202), channel_id=1, source_target_pairs={{0,1},{1,2},{2,3},{3,4},{4,5},{5,6},{6,7},{7,8},{8,9},{9,10},{10,1... | collective-permute-start | bytes 34568 | tf_op jit(solution)/shard_map/ppermute | solution.py:27
  151.3 1.9 collective-permute-start.5
  153.2 4.3 pad_add_fusion
  158.3 1.9 collective-permute-start.10
  161.3 2.1 copy.205
  163.4 2.7 pad_maximum_fusion.1
  167.6 12.4 %copy.210 = bf16[1,26,6,66,40]{4,0,3,2,1:T(2,128)(2,1)} copy(bf16[1,26,6,66,40]{3,4,2,1,0:T(8,128)(2,1)} %pad_bitcast_fusion) | data formatting | bytes 1647360 | tf_op jit(solution)/shard_map/broadcast_in_dim | solution.py:82
  180.0 42.7 %fusion.252 = f32[3,3,3,40,32]{3,4,2,1,0:T(8,128)} fusion(bf16[1,26,6,66,40]{4,0,3,2,1:T(2,128)(2,1)} %copy.210, bf16[1,24,4,64,32]{4,0,3,2,1:T(2,128)(2,1)} %copy.211), kind=kOutput, calls=%fused_computation.321 | convolution fusion | flops 424673280 | bytes 1355136 | tf_op jit(solution)/shard_map/transpose | solution.py:89
  222.7 3.9 fusion.257
  226.6 3.3 copy.290
  230.9 6.0 %select_convert_fusion.1 = bf16[24,4,8,9,32]{4,2,3,1,0:T(8,128)(2,1)S(1)} fusion(pred[8,9]{0,1:T(8,128)(4,1)S(1)} %copy-done.29, bf16[3,3,3,40,32]{3,4,2,1,0:T(8,128)(2,1)S(1)} %copy-done, bf16[24,6,1,7,2,40]{5,3,4,1,0,2:T(8,128)(2,1)S(1)} %slice.373, bf16[24,6,1,8,9,40]{5,3,4,1,0,2:T(8,128)(2,1)S(1)} %copy.208), kind=kOutput, calls=%fused_computation.53 | convolution fusion | flops 467970048 | bytes 1502280 | tf_op jit(solution)/shard_map/conv_general_dilated | solution.py:37
  238.1 1.8 slice_add_fusion.1
  240.0 1.9 collective-permute-start.11
  243.8 237.6 %all-reduce.27.cloned.1.call-done = f32[3,3,3,40,32]{3,4,2,1,0:T(8,128)} async-done(((f32[3,3,3,40,32]{3,4,2,1,0:T(8,128)}), f32[3,3,3,40,32]{3,4,2,1,0:T(8,128)}) %all-reduce.27.cloned.1.call-update) | async-done | bytes 138256 | tf_op jit(solution)/shard_map/psum | solution.py:91
  481.5 1.8 broadcast_multiply_fusion
  483.3 1.8 fusion.70
  (217 shorter events, 81.3 us)
Async XLA Ops:
  7.2 36.9 %copy-start = (bf16[3,3,3,40,32]{3,4,2,1,0:T(8,128)(2,1)S(1)}, bf16[3,3,3,40,32]{3,4,2,1,0:T(8,128)(2,1)}, u32[]{:S(2)}) copy-start(bf16[3,3,3,40,32]{3,4,2,1,0:T(8,128)(2,1)} %param.6) | copy-start | bytes 207364
  7.2 7.6 %copy-start.27 = (bf16[4,64,320]{2,1,0:T(8,128)(2,1)S(1)}, bf16[4,64,320]{2,1,0:T(8,128)(2,1)}, u32[]{:S(2)}) copy-start(bf16[4,64,320]{2,1,0:T(8,128)(2,1)} %param.5) | copy-start | bytes 491524
  7.2 474.3 %all-reduce.27.cloned.1.call-start = ((), (), s32[]{:S(2)}) async-start(), calls=%async_computation | async-start | bytes 884736 | tf_op jit(solution)/shard_map/psum | solution.py:91
  9.2 25.1 %copy-start.1 = (bf16[4,64,320]{2,1,0:T(8,128)(2,1)S(1)}, bf16[4,64,320]{2,1,0:T(8,128)(2,1)}, u32[]{:S(2)}) copy-start(bf16[4,64,320]{2,1,0:T(8,128)(2,1)} %param.4) | copy-start | bytes 491524
  9.2 26.2 %copy-start.4 = (bf16[24,4,64,32]{2,3,1,0:T(8,128)(2,1)S(1)}, bf16[24,4,64,32]{2,3,1,0:T(8,128)(2,1)}, u32[]{:S(2)}) copy-start(bf16[24,4,64,32]{2,3,1,0:T(8,128)(2,1)} %param.7) | copy-start | bytes 1179652
  9.3 11.8 %collective-permute-start.6 = (bf16[24,1,64,32]{3,0,2,1:T(8,128)(2,1)S(1)}, bf16[24,1,64,32]{3,0,2,1:T(8,128)(2,1)S(1)}, u32[]{:S(2)}, u32[]{:S(2)}) collective-permute-start(bf16[24,1,64,32]{3,0,2,1:T(8,128)(2,1)S(1)} %get-tuple-element.46), channel_id=1, source_target_pairs={{0,32},{32,64},{64,96},{96,128},{128,160},{160,192},{192,224},{1,3... | collective-permute-start | bytes 294920 | tf_op jit(solution)/shard_map/ppermute | solution.py:27
  13.4 11.6 %collective-permute-start.7 = (bf16[24,1,64,32]{3,0,2,1:T(8,128)(2,1)S(1)}, bf16[24,1,64,32]{3,0,2,1:T(8,128)(2,1)S(1)}, u32[]{:S(2)}, u32[]{:S(2)}) collective-permute-start(bf16[24,1,64,32]{3,0,2,1:T(8,128)(2,1)S(1)} %get-tuple-element.47), channel_id=1, source_target_pairs={{32,0},{64,32},{96,64},{128,96},{160,128},{192,160},{224,192},{33,... | collective-permute-start | bytes 294920 | tf_op jit(solution)/shard_map/ppermute | solution.py:29
  14.7 90.8 %collective-permute-start = (bf16[4,64,320]{2,1,0:T(8,128)(2,1)S(1)}, bf16[4,64,320]{2,1,0:T(8,128)(2,1)}, u32[]{:S(2)}, u32[]{:S(2)}) collective-permute-start(bf16[4,64,320]{2,1,0:T(8,128)(2,1)S(1)} %copy-done.27), channel_id=1, source_target_pairs={{0,1},{1,2},{2,3},{3,4},{4,5},{5,6},{6,7},{7,8},{8,9},{9,10},{10,1... | collective-permute-start | bytes 491528 | tf_op jit(solution)/shard_map/ppermute | solution.py:16
  25.8 14.8 %collective-permute-start.8 = (bf16[24,6,1,32]{3,0,2,1:T(8,128)(2,1)S(1)}, bf16[24,6,1,32]{3,0,2,1:T(8,128)(2,1)S(1)}, u32[]{:S(2)}, u32[]{:S(2)}) collective-permute-start(bf16[24,6,1,32]{3,0,2,1:T(8,128)(2,1)S(1)} %get-tuple-element.20), channel_id=1, source_target_pairs={{0,1},{1,2},{2,3},{3,4},{4,5},{5,6},{6,7},{7,8},{8,9},{9,10},{10,1... | collective-permute-start | bytes 27656 | tf_op jit(solution)/shard_map/ppermute | solution.py:27
  32.3 8.2 %collective-permute-start.9 = (bf16[24,6,1,32]{3,0,2,1:T(8,128)(2,1)S(1)}, bf16[24,6,1,32]{3,0,2,1:T(8,128)(2,1)S(1)}, u32[]{:S(2)}, u32[]{:S(2)}) collective-permute-start(bf16[24,6,1,32]{3,0,2,1:T(8,128)(2,1)S(1)} %get-tuple-element.21), channel_id=1, source_target_pairs={{1,0},{2,1},{3,2},{4,3},{5,4},{6,5},{7,6},{8,7},{9,8},{10,9},{11,1... | collective-permute-start | bytes 27656 | tf_op jit(solution)/shard_map/ppermute | solution.py:29
  52.9 46.2 %copy-start.6 = (f32[4,64,320]{2,1,0:T(8,128)}, f32[4,64,320]{2,1,0:T(8,128)S(1)}, u32[]{:S(2)}) copy-start(f32[4,64,320]{2,1,0:T(8,128)S(1)} %fusion.112) | copy-start | bytes 983044
  53.3 45.8 %copy-start.8 = (f32[4,64,320]{2,1,0:T(8,128)}, f32[4,64,320]{2,1,0:T(8,128)S(1)}, u32[]{:S(2)}) copy-start(f32[4,64,320]{2,1,0:T(8,128)S(1)} %fusion.114) | copy-start | bytes 983044
  53.8 45.3 %copy-start.10 = (f32[4,64,320]{2,1,0:T(8,128)}, f32[4,64,320]{2,1,0:T(8,128)S(1)}, u32[]{:S(2)}) copy-start(f32[4,64,320]{2,1,0:T(8,128)S(1)} %fusion.116) | copy-start | bytes 983044
  105.2 9.5 %copy-start.5 = (f32[24,4,64,40]{2,3,1,0:T(8,128)S(1)}, f32[24,4,64,40]{2,3,1,0:T(8,128)}, u32[]{:S(2)}) copy-start(f32[24,4,64,40]{2,3,1,0:T(8,128)} %fusion.45) | copy-start | bytes 2949124
  105.5 8.2 %collective-permute-start.1 = (bf16[4,64,320]{2,1,0:T(8,128)(2,1)}, bf16[4,64,320]{2,1,0:T(8,128)(2,1)S(1)}, u32[]{:S(2)}, u32[]{:S(2)}) collective-permute-start(bf16[4,64,320]{2,1,0:T(8,128)(2,1)} %collective-permute-done), channel_id=1, source_target_pairs={{0,1},{1,2},{2,3},{3,4},{4,5},{5,6},{6,7},{7,8},{8,9},{9,10},{10,1... | collective-permute-start | bytes 491528 | tf_op jit(solution)/shard_map/ppermute | solution.py:16
  124.4 8.2 %copy-start.28 = (bf16[4,64,320]{2,1,0:T(8,128)(2,1)S(1)}, bf16[4,64,320]{2,1,0:T(8,128)(2,1)}, u32[]{:S(2)}) copy-start(bf16[4,64,320]{2,1,0:T(8,128)(2,1)} %param.5) | copy-start | bytes 491524
  124.9 7.7 %copy-start.26 = (f32[4,64,320]{2,1,0:T(8,128)S(1)}, f32[4,64,320]{2,1,0:T(8,128)}, u32[]{:S(2)}) copy-start(f32[4,64,320]{2,1,0:T(8,128)} %fusion.104) | copy-start | bytes 983044
  125.5 7.1 %copy-start.25 = (f32[4,64,320]{2,1,0:T(8,128)S(1)}, f32[4,64,320]{2,1,0:T(8,128)}, u32[]{:S(2)}) copy-start(f32[4,64,320]{2,1,0:T(8,128)} %fusion.102) | copy-start | bytes 983044
  126.0 6.6 %copy-start.22 = (f32[4,64,320]{2,1,0:T(8,128)S(1)}, f32[4,64,320]{2,1,0:T(8,128)}, u32[]{:S(2)}) copy-start(f32[4,64,320]{2,1,0:T(8,128)} %fusion.138) | copy-start | bytes 983044
  126.0 6.6 %copy-start.24 = (f32[4,64,320]{2,1,0:T(8,128)S(1)}, f32[4,64,320]{2,1,0:T(8,128)}, u32[]{:S(2)}) copy-start(f32[4,64,320]{2,1,0:T(8,128)} %fusion.100) | copy-start | bytes 983044
  126.5 6.1 %copy-start.21 = (f32[4,64,320]{2,1,0:T(8,128)S(1)}, f32[4,64,320]{2,1,0:T(8,128)}, u32[]{:S(2)}) copy-start(f32[4,64,320]{2,1,0:T(8,128)} %fusion.136) | copy-start | bytes 983044
  127.1 5.6 %copy-start.19 = (f32[4,64,320]{2,1,0:T(8,128)S(1)}, f32[4,64,320]{2,1,0:T(8,128)}, u32[]{:S(2)}) copy-start(f32[4,64,320]{2,1,0:T(8,128)} %fusion.132) | copy-start | bytes 983044
  127.1 5.6 %copy-start.20 = (f32[4,64,320]{2,1,0:T(8,128)S(1)}, f32[4,64,320]{2,1,0:T(8,128)}, u32[]{:S(2)}) copy-start(f32[4,64,320]{2,1,0:T(8,128)} %fusion.134) | copy-start | bytes 983044
  127.6 5.1 %copy-start.7 = (f32[4,64,320]{2,1,0:T(8,128)S(1)}, f32[4,64,320]{2,1,0:T(8,128)}, u32[]{:S(2)}) copy-start(f32[4,64,320]{2,1,0:T(8,128)} %copy-done.6) | copy-start | bytes 983044
  127.6 5.1 %copy-start.9 = (f32[4,64,320]{2,1,0:T(8,128)S(1)}, f32[4,64,320]{2,1,0:T(8,128)}, u32[]{:S(2)}) copy-start(f32[4,64,320]{2,1,0:T(8,128)} %copy-done.8) | copy-start | bytes 983044
  127.6 5.1 %copy-start.11 = (f32[4,64,320]{2,1,0:T(8,128)S(1)}, f32[4,64,320]{2,1,0:T(8,128)}, u32[]{:S(2)}) copy-start(f32[4,64,320]{2,1,0:T(8,128)} %copy-done.10) | copy-start | bytes 983044
  127.9 9.3 %collective-permute-start.2 = (bf16[24,1,64,40]{2,3,1,0:T(8,128)(2,1)S(1)}, bf16[24,1,64,40]{2,3,1,0:T(8,128)(2,1)S(1)}, u32[]{:S(2)}, u32[]{:S(2)}) collective-permute-start(bf16[24,1,64,40]{2,3,1,0:T(8,128)(2,1)S(1)} %get-tuple-element.50), channel_id=1, source_target_pairs={{0,32},{32,64},{64,96},{96,128},{128,160},{160,192},{192,224},{1,3... | collective-permute-start | bytes 368648 | tf_op jit(solution)/shard_map/ppermute | solution.py:27
  131.3 6.9 %collective-permute-start.3 = (bf16[24,1,64,40]{2,3,1,0:T(8,128)(2,1)S(1)}, bf16[24,1,64,40]{2,3,1,0:T(8,128)(2,1)S(1)}, u32[]{:S(2)}, u32[]{:S(2)}) collective-permute-start(bf16[24,1,64,40]{2,3,1,0:T(8,128)(2,1)S(1)} %get-tuple-element.51), channel_id=1, source_target_pairs={{32,0},{64,32},{96,64},{128,96},{160,128},{192,160},{224,192},{33,... | collective-permute-start | bytes 368648 | tf_op jit(solution)/shard_map/ppermute | solution.py:29
  142.7 17.6 %collective-permute-start.4 = (bf16[24,6,1,40]{3,0,2,1:T(8,128)(2,1)S(1)}, bf16[24,6,1,40]{3,0,2,1:T(8,128)(2,1)S(1)}, u32[]{:S(2)}, u32[]{:S(2)}) collective-permute-start(bf16[24,6,1,40]{3,0,2,1:T(8,128)(2,1)S(1)} %copy.202), channel_id=1, source_target_pairs={{0,1},{1,2},{2,3},{3,4},{4,5},{5,6},{6,7},{7,8},{8,9},{9,10},{10,1... | collective-permute-start | bytes 34568 | tf_op jit(solution)/shard_map/ppermute | solution.py:27
  151.3 10.0 %collective-permute-start.5 = (bf16[24,6,1,40]{3,0,2,1:T(8,128)(2,1)S(1)}, bf16[24,6,1,40]{3,0,2,1:T(8,128)(2,1)S(1)}, u32[]{:S(2)}, u32[]{:S(2)}) collective-permute-start(bf16[24,6,1,40]{3,0,2,1:T(8,128)(2,1)S(1)} %copy.203), channel_id=1, source_target_pairs={{1,0},{2,1},{3,2},{4,3},{5,4},{6,5},{7,6},{8,7},{9,8},{10,9},{11,1... | collective-permute-start | bytes 34568 | tf_op jit(solution)/shard_map/ppermute | solution.py:29
  158.3 79.3 %collective-permute-start.10 = (f32[4,64,320]{2,1,0:T(8,128)}, f32[4,64,320]{2,1,0:T(8,128)}, u32[]{:S(2)}, u32[]{:S(2)}) collective-permute-start(f32[4,64,320]{2,1,0:T(8,128)} %slice.426), channel_id=1, source_target_pairs={{1,0},{2,1},{3,2},{4,3},{5,4},{6,5},{7,6},{8,7},{9,8},{10,9},{11,1... | collective-permute-start | bytes 983048 | tf_op jit(solution)/shard_map/ppermute | solution.py:16
  240.0 243.3 %collective-permute-start.11 = (f32[4,64,320]{2,1,0:T(8,128)}, f32[4,64,320]{2,1,0:T(8,128)}, u32[]{:S(2)}, u32[]{:S(2)}) collective-permute-start(f32[4,64,320]{2,1,0:T(8,128)} %slice_add_fusion.1), channel_id=1, source_target_pairs={{1,0},{2,1},{3,2},{4,3},{5,4},{6,5},{7,6},{8,7},{9,8},{10,9},{11,1... | collective-permute-start | bytes 983048 | tf_op jit(solution)/shard_map/ppermute | solution.py:16
  (11 other events, 41.1 us)
Sparse Core Ops, SparseCore 0:
  222.9 258.5 all-reduce.26
where the time goes:
time: 497 us; the launch traced here: 492 us
  waiting for transfers between devices  245 us (49%)
  matrix products  93 us (19%)
  local copies, waits for them, and re-layouts  74 us (15%)
  starting transfers between devices  43.3 us (9%)
  other arithmetic  20.8 us (4%)
  between operations  15.6 us (3%)
    psum x1, waiting for transfers between devices, on_device(): weight_grad = lax.psum(local_grad, ('row', 'col')) / math.sqrt(total_cells)  238 us
    transpose x1, matrix products, on_device(): local_grad = jnp.transpose(kernel_raw, (1, 2, 3, 0, 4))  42.7 us
    dot_general x24, matrix products, on_device(): jnp.einsum('hwg,cg->hwc', grad_volume[disp_index].astype(jnp.float32), gr...  25.2 us
    ppermute x4, starting transfers between devices, with_halo(): lax.ppermute(tail, axis, [(i, (i + 1) % count) for i in range(ends)])  21.7 us
    convert_element_type x50, local copies, waits for them, and re-layouts, on_device(): grad_volume = conv_valid(padded_cotangent, flipped).astype(jnp.bfloat16)  21.1 us
    unnamed x88, local copies, waits for them, and re-layouts  20.9 us
    ppermute x4, starting transfers between devices, shifted_2(): return lax.ppermute(block, axis, route)  15.2 us
    broadcast_in_dim x2, local copies, waits for them, and re-layouts, on_device(): full_pad[None]  13.9 us
  transfers between devices with their start and end apart: 13, of which 5 were waited for; matrix products, arithmetic and copies ran while one was open for 33% of the time, Pallas kernels for 0%

commit v1 on v0

--- a/solution.py
+++ b/solution.py
@@ -88,7 +88,9 @@
     )
     local_grad = jnp.transpose(kernel_raw, (1, 2, 3, 0, 4))
     total_cells = DISP * tile_rows * lax.axis_size("row") * tile_cols * lax.axis_size("col")
-    weight_grad = lax.psum(local_grad, ("row", "col")) / math.sqrt(total_cells)
+    weight_grad = jnp.sum(lax.all_gather(local_grad, ("row", "col")), axis=0) / math.sqrt(
+        total_cells
+    )
     left_accum = jnp.zeros((tile_rows, tile_cols, channels), jnp.float32)
     grad_band = jnp.zeros((tile_rows, band_width, channels), jnp.float32)
     for disp_index in range(DISP):

time: 497 us -> 826 us (1.66); the launches traced: 492 us -> 812 us
  waiting for transfers between devices: 245 us -> 572 us
  other arithmetic: 20.8 us -> 54 us
  local copies, waits for them, and re-layouts: 74 us -> 50 us
  matrix products: 93 us -> 76.5 us
    all_gather x0 -> x1, waiting for transfers between devices: none -> 535 us  [on_device(): lax.all_gather(local_grad, ('row', 'col'))]
    psum x1 -> x0, waiting for transfers between devices: 238 us -> none  [on_device(): weight_grad = lax.psum(local_grad, ('row', 'col')) / math.sqrt(total_cells)]
    reduce_sum x0 -> x1, other arithmetic: none -> 34.4 us  [on_device(): jnp.sum(lax.all_gather(local_grad, ('row', 'col')), axis=0)]
    ppermute x4, waiting for transfers between devices: 2.27 us -> 23.1 us  [shifted_2(): return lax.ppermute(block, axis, route)]
    convert_element_type x50, local copies, waits for them, and re-layouts: 21.1 us -> 2.5 us  [on_device(): grad_volume = conv_valid(padded_cotangent, flipped).astype(jnp.bfloat16)]
    dot_general x24, matrix products: 25.2 us -> 8.38 us  [on_device(): jnp.einsum('hwg,cg->hwc', grad_volume[disp_index].astype(jnp.float32), gr...]
    unnamed x88 -> x64, local copies, waits for them, and re-layouts: 20.9 us -> 11.6 us
  transfers between devices with their start and end apart: 13 -> 13, of which waited for: 5 -> 10; matrix products, arithmetic and copies ran while one was open for 33% -> 8% of each run, Pallas kernels for 0% -> 0%
where the time goes in v1:
time: 826 us; the launch traced here: 812 us
  waiting for transfers between devices  572 us (69%)
  matrix products  76.5 us (9%)
  other arithmetic  54 us (7%)
  local copies, waits for them, and re-layouts  50 us (6%)
  starting transfers between devices  43.9 us (5%)
  between operations  15.8 us (2%)
    all_gather x1, waiting for transfers between devices, on_device(): lax.all_gather(local_grad, ('row', 'col'))  535 us
    transpose x1, matrix products, on_device(): local_grad = jnp.transpose(kernel_raw, (1, 2, 3, 0, 4))  42.7 us
    reduce_sum x1, other arithmetic, on_device(): jnp.sum(lax.all_gather(local_grad, ('row', 'col')), axis=0)  34.4 us
    ppermute x4, waiting for transfers between devices, shifted_2(): return lax.ppermute(block, axis, route)  23.1 us
    ppermute x4, starting transfers between devices, with_halo(): lax.ppermute(tail, axis, [(i, (i + 1) % count) for i in range(ends)])  21.5 us
  transfers between devices with their start and end apart: 13, of which 10 were waited for; matrix products, arithmetic and copies ran while one was open for 8% of the time, Pallas kernels for 0%

profile of v1, /device:TPU:1, one launch (start us, length us, event | category | flops | bytes accessed | tf_op | source)
XLA Modules:
  0.0 812.0 jit_solution(5889189941326507318)
XLA Ops:
  7.2 6.3 collective-permute-start
  13.6 2.9 collective-permute-done
  16.5 5.8 collective-permute-start.1
  40.4 4.0 collective-permute-start.2
  48.5 1.8 fusion.250
  50.4 2.3 copy.203
  52.7 1.9 collective-permute-start.5
  55.5 7.4 collective-permute-start.4
  62.9 7.3 copy.211
  71.2 2.0 copy.204
  73.2 3.0 pad_maximum_fusion.1
  77.7 12.4 %copy.210 = bf16[1,26,6,66,40]{4,0,3,2,1:T(2,128)(2,1)} copy(bf16[1,26,6,66,40]{3,4,2,1,0:T(8,128)(2,1)} %pad_bitcast_fusion) | data formatting | bytes 1647360 | tf_op jit(solution)/shard_map/broadcast_in_dim | solution.py:82
  90.1 42.7 %fusion.252 = f32[3,3,3,40,32]{3,4,2,1,0:T(8,128)} fusion(bf16[1,26,6,66,40]{4,0,3,2,1:T(2,128)(2,1)} %copy.210, bf16[1,24,4,64,32]{4,0,3,2,1:T(2,128)(2,1)} %copy.211), kind=kOutput, calls=%fused_computation.321 | convolution fusion | flops 424673280 | bytes 1355136 | tf_op jit(solution)/shard_map/transpose | solution.py:89
  132.8 1.9 copy.212
  136.1 4.8 collective-permute-start.6
  140.9 3.2 collective-permute-done.7
  145.6 1.9 collective-permute-start.9
  147.5 5.4 collective-permute-start.8
  152.9 5.8 collective-permute-done.9
  158.7 10.2 %maximum_bitcast_fusion = bf16[24,6,1,66,32]{4,0,3,1,2:T(8,128)(2,1)S(1)} fusion(bf16[24,6,1,32]{3,0,2,1:T(8,128)(2,1)S(1)} %collective-permute-done.9, bf16[24,1,64,32]{3,0,2,1:T(8,128)(2,1)S(1)} %collective-permute-done.7, bf16[24,4,64,32]{3,0,2,1:T(8,128)(2,1)S(1)} %copy.212, bf16[24,1,64,32]{3,0,2,1:T(8,128)(2,1)S(1)} %collective-permute-done.6, ...), kind=kLoop, calls=%fused_computation.66 | loop fusion | flops 1216512 | bytes 1216512 | tf_op jit(solution)/shard_map/broadcast_in_dim | solution.py:38
  170.0 5.4 select_convert_fusion
  188.6 2.3 multiply_convert_fusion.1
  193.4 1.9 collective-permute-start.10
  196.7 2.8 copy.290
  199.5 2.2 pad.125.clone
  202.2 10.5 %collective-permute-done.10 = f32[4,64,320]{2,1,0:T(8,128)} collective-permute-done((f32[4,64,320]{2,1,0:T(8,128)}, f32[4,64,320]{2,1,0:T(8,128)}, u32[]{:S(2)}, u32[]{:S(2)}) %collective-permute-start.10) | collective-permute-done | bytes 327712 | tf_op jit(solution)/shard_map/ppermute | solution.py:16
  212.7 1.8 slice_add_fusion.1
  214.5 1.9 collective-permute-start.11
  216.4 6.0 select_convert_fusion.1
  225.1 8.6 %collective-permute-done.11 = f32[4,64,320]{2,1,0:T(8,128)S(1)} collective-permute-done((f32[4,64,320]{2,1,0:T(8,128)}, f32[4,64,320]{2,1,0:T(8,128)S(1)}, u32[]{:S(2)}, u32[]{:S(2)}) %collective-permute-start.11) | collective-permute-done | bytes 327712 | tf_op jit(solution)/shard_map/ppermute | solution.py:16
  234.4 535.1 %all-gather.3.cloned.1.call-done = f32[768,3,3,40,32]{3,4,2,1,0:T(8,128)} async-done(((f32[3,3,3,40,32]{3,4,2,1,0:T(8,128)}), f32[768,3,3,40,32]{3,4,2,1,0:T(8,128)}) %all-gather.3.cloned.1.call-update) | async-done | bytes 35389456 | tf_op jit(solution)/shard_map/all_gather | solution.py:91
  769.6 34.4 %reduce_sum.9 = f32[3,3,3,40,32]{3,4,2,1,0:T(8,128)S(1)} reduce(f32[256,3,3,3,40,32]{4,5,3,2,1,0:T(8,128)} %bitcast.32, f32[]{:T(128)} %constant.31.clone.1), dimensions={0}, to_apply=%region_0.1 | reduce | flops 8812800 | bytes 35527684 | tf_op jit(solution)/shard_map/reduce_sum | solution.py:91
  (194 shorter events, 50.4 us)
Async XLA Ops:
  7.2 162.7 %copy-start = (bf16[3,3,3,40,32]{3,4,2,1,0:T(8,128)(2,1)S(1)}, bf16[3,3,3,40,32]{3,4,2,1,0:T(8,128)(2,1)}, u32[]{:S(2)}) copy-start(bf16[3,3,3,40,32]{3,4,2,1,0:T(8,128)(2,1)} %param.6) | copy-start | bytes 207364
  7.2 20.4 %copy-start.1 = (bf16[4,64,320]{2,1,0:T(8,128)(2,1)S(1)}, bf16[4,64,320]{2,1,0:T(8,128)(2,1)}, u32[]{:S(2)}) copy-start(bf16[4,64,320]{2,1,0:T(8,128)(2,1)} %param.4) | copy-start | bytes 491524
  7.2 762.4 %all-gather.3.cloned.1.call-start = ((), (), s32[]{:S(2)}) async-start(), calls=%async_computation | async-start | bytes 113688576 | tf_op jit(solution)/shard_map/all_gather | solution.py:91
  7.2 9.3 %collective-permute-start = (bf16[4,64,320]{2,1,0:T(8,128)(2,1)}, bf16[4,64,320]{2,1,0:T(8,128)(2,1)S(1)}, u32[]{:S(2)}, u32[]{:S(2)}) collective-permute-start(bf16[4,64,320]{2,1,0:T(8,128)(2,1)} %param.5), channel_id=1, source_target_pairs={{0,1},{1,2},{2,3},{3,4},{4,5},{5,6},{6,7},{7,8},{8,9},{9,10},{10,1... | collective-permute-start | bytes 491528 | tf_op jit(solution)/shard_map/ppermute | solution.py:16
  16.5 18.2 %copy-start.15 = (bf16[4,64,320]{2,1,0:T(8,128)(2,1)}, bf16[4,64,320]{2,1,0:T(8,128)(2,1)S(1)}, u32[]{:S(2)}) copy-start(bf16[4,64,320]{2,1,0:T(8,128)(2,1)S(1)} %collective-permute-done) | copy-start | bytes 491524
  16.5 8.4 %collective-permute-start.1 = (bf16[4,64,320]{2,1,0:T(8,128)(2,1)S(1)}, bf16[4,64,320]{2,1,0:T(8,128)(2,1)S(1)}, u32[]{:S(2)}, u32[]{:S(2)}) collective-permute-start(bf16[4,64,320]{2,1,0:T(8,128)(2,1)S(1)} %collective-permute-done), channel_id=1, source_target_pairs={{0,1},{1,2},{2,3},{3,4},{4,5},{5,6},{6,7},{7,8},{8,9},{9,10},{10,1... | collective-permute-start | bytes 491528 | tf_op jit(solution)/shard_map/ppermute | solution.py:16
  25.0 13.3 %copy-start.12 = (bf16[4,128,320]{2,1,0:T(8,128)(2,1)}, bf16[4,128,320]{2,1,0:T(8,128)(2,1)S(1)}, u32[]{:S(2)}) copy-start(bf16[4,128,320]{2,1,0:T(8,128)(2,1)S(1)} %get-tuple-element.76) | copy-start | bytes 983044
  39.1 6.9 collective-permute-start.3
  40.4 7.1 collective-permute-start.2
  46.0 1.5 copy-start.7
  47.5 0.7 copy-start.9
  52.7 17.5 %collective-permute-start.5 = (bf16[24,6,1,40]{3,0,2,1:T(8,128)(2,1)S(1)}, bf16[24,6,1,40]{3,0,2,1:T(8,128)(2,1)S(1)}, u32[]{:S(2)}, u32[]{:S(2)}) collective-permute-start(bf16[24,6,1,40]{3,0,2,1:T(8,128)(2,1)S(1)} %copy.203), channel_id=1, source_target_pairs={{1,0},{2,1},{3,2},{4,3},{5,4},{6,5},{7,6},{8,7},{9,8},{10,9},{11,1... | collective-permute-start | bytes 34568 | tf_op jit(solution)/shard_map/ppermute | solution.py:29
  55.5 15.7 %collective-permute-start.4 = (bf16[24,6,1,40]{3,0,2,1:T(8,128)(2,1)S(1)}, bf16[24,6,1,40]{3,0,2,1:T(8,128)(2,1)S(1)}, u32[]{:S(2)}, u32[]{:S(2)}) collective-permute-start(bf16[24,6,1,40]{3,0,2,1:T(8,128)(2,1)S(1)} %copy.202), channel_id=1, source_target_pairs={{0,1},{1,2},{2,3},{3,4},{4,5},{5,6},{6,7},{7,8},{8,9},{9,10},{10,1... | collective-permute-start | bytes 34568 | tf_op jit(solution)/shard_map/ppermute | solution.py:27
  71.2 5.0 copy-start.2
  134.8 9.3 %collective-permute-start.7 = (bf16[24,1,64,32]{3,0,2,1:T(8,128)(2,1)S(1)}, bf16[24,1,64,32]{3,0,2,1:T(8,128)(2,1)S(1)}, u32[]{:S(2)}, u32[]{:S(2)}) collective-permute-start(bf16[24,1,64,32]{3,0,2,1:T(8,128)(2,1)S(1)} %get-tuple-element.47), channel_id=1, source_target_pairs={{32,0},{64,32},{96,64},{128,96},{160,128},{192,160},{224,192},{33,... | collective-permute-start | bytes 294920 | tf_op jit(solution)/shard_map/ppermute | solution.py:29
  136.1 9.4 %collective-permute-start.6 = (bf16[24,1,64,32]{3,0,2,1:T(8,128)(2,1)S(1)}, bf16[24,1,64,32]{3,0,2,1:T(8,128)(2,1)S(1)}, u32[]{:S(2)}, u32[]{:S(2)}) collective-permute-start(bf16[24,1,64,32]{3,0,2,1:T(8,128)(2,1)S(1)} %get-tuple-element.46), channel_id=1, source_target_pairs={{0,32},{32,64},{64,96},{96,128},{128,160},{160,192},{192,224},{1,3... | collective-permute-start | bytes 294920 | tf_op jit(solution)/shard_map/ppermute | solution.py:27
  145.6 13.1 %collective-permute-start.9 = (bf16[24,6,1,32]{3,0,2,1:T(8,128)(2,1)S(1)}, bf16[24,6,1,32]{3,0,2,1:T(8,128)(2,1)S(1)}, u32[]{:S(2)}, u32[]{:S(2)}) collective-permute-start(bf16[24,6,1,32]{3,0,2,1:T(8,128)(2,1)S(1)} %get-tuple-element.21), channel_id=1, source_target_pairs={{1,0},{2,1},{3,2},{4,3},{5,4},{6,5},{7,6},{8,7},{9,8},{10,9},{11,1... | collective-permute-start | bytes 27656 | tf_op jit(solution)/shard_map/ppermute | solution.py:29
  147.5 11.2 %collective-permute-start.8 = (bf16[24,6,1,32]{3,0,2,1:T(8,128)(2,1)S(1)}, bf16[24,6,1,32]{3,0,2,1:T(8,128)(2,1)S(1)}, u32[]{:S(2)}, u32[]{:S(2)}) collective-permute-start(bf16[24,6,1,32]{3,0,2,1:T(8,128)(2,1)S(1)} %get-tuple-element.20), channel_id=1, source_target_pairs={{0,1},{1,2},{2,3},{3,4},{4,5},{5,6},{6,7},{7,8},{8,9},{9,10},{10,1... | collective-permute-start | bytes 27656 | tf_op jit(solution)/shard_map/ppermute | solution.py:27
  169.4 0.7 copy-start.17
  175.4 1.2 copy-start.11
  187.4 1.0 copy-start.13
  187.5 1.1 copy-start.14
  187.5 1.2 copy-start.16
  191.2 4.1 copy-start.3
  191.2 4.1 copy-start.4
  191.2 4.1 copy-start.8
  191.2 4.1 copy-start.10
  192.2 1.2 copy-start.5
  193.4 19.3 %collective-permute-start.10 = (f32[4,64,320]{2,1,0:T(8,128)}, f32[4,64,320]{2,1,0:T(8,128)}, u32[]{:S(2)}, u32[]{:S(2)}) collective-permute-start(f32[4,64,320]{2,1,0:T(8,128)} %slice.426), channel_id=1, source_target_pairs={{1,0},{2,1},{3,2},{4,3},{5,4},{6,5},{7,6},{8,7},{9,8},{10,9},{11,1... | collective-permute-start | bytes 983048 | tf_op jit(solution)/shard_map/ppermute | solution.py:16
  201.7 11.0 %copy-start.6 = (f32[4,192,320]{2,1,0:T(8,128)S(1)}, f32[4,192,320]{2,1,0:T(8,128)}, u32[]{:S(2)}) copy-start(f32[4,192,320]{2,1,0:T(8,128)} %copy-done.5) | copy-start | bytes 2949124
  214.5 19.2 %collective-permute-start.11 = (f32[4,64,320]{2,1,0:T(8,128)}, f32[4,64,320]{2,1,0:T(8,128)S(1)}, u32[]{:S(2)}, u32[]{:S(2)}) collective-permute-start(f32[4,64,320]{2,1,0:T(8,128)} %slice_add_fusion.1), channel_id=1, source_target_pairs={{1,0},{2,1},{3,2},{4,3},{5,4},{6,5},{7,6},{8,7},{9,8},{10,9},{11,1... | collective-permute-start | bytes 983048 | tf_op jit(solution)/shard_map/ppermute | solution.py:16
Sparse Core Ops, SparseCore 0:
  132.9 636.5 all-gather.2
